TPU v7x, 512 devices: a whole 4x8x8 slice. The times are simulated.
512 devices in a mesh: rep: 64 (over z_lo, y, core), tp: 8 (over x, z_hi).
Axes of the slice: x: 4, y: 8, z: 8 (z_hi: 2, z_lo: 4; z = z_hi * 4 + z_lo), core: 2. Of those that a mesh axis runs over, the one named last changes fastest.
Arguments:
- activations: bfloat16 [64, 1024, 256], P('rep', 'tp'), may hold values from -6 to 6
- out_grads: bfloat16 [64, 1024, 4096], P('rep', None, 'tp'), may hold values from -6 to 6
- weight: bfloat16 [64, 256, 4096], P('rep', None, 'tp'), may hold values from -6 to 6
- public: bfloat16 [64, 256, 4096], P('rep', None, 'tp'), may hold values from -6 to 6
- counts: int32 [64], P('rep'), may hold values from 256 to 1024, as said below
- kept: int32 [64, 8, 40], P('rep', 'tp'), may hold values from 0 to 63, as said below
- distances: int32 [2], replicated, may hold values from 1 to 32, as said below
Outputs:
- new_weight: bfloat16 [64, 256, 4096], P('rep', None, 'tp')
Inputs may be any that keep to these rules, and one draw needn't show every extreme that they name: `counts`: at least 256; some replica has exactly 1024. `kept`: the 40 indices of each replica and shard are distinct. `distances`: powers of two, the same for every replica; the rounds' distances differ, and one of the rounds has distance half the number of replicas.
All inputs are finite; a program needn't handle non-finite values.
Results may differ from a plain program's by a relative error of at most 0.006.
Values may be sent and summed in bfloat16 or wider, within the bound.
No kernel may reach another device: no remote copies, remote signals or barrier semaphores. Data moves between devices by JAX's collectives and lax.ppermute only.
A program may use at most 128 MiB of HBM per device.

v0:
```python
import jax
import jax.numpy as jnp
import numpy as np
from jax import lax
from jax.experimental import pallas as pl
from jax.experimental.pallas import tpu as pltpu
from jax.sharding import PartitionSpec as P


learn_rate = 0.02
step = 0.25
ROWS, COLS, KEEP, SLABS, TOP = 256, 512, 40, 64, 5
LEFT = SLABS - KEEP
PACKED = (2, 3, TOP)
f32, bf16, i32 = jnp.float32, jnp.bfloat16, jnp.int32
VM = pl.BlockSpec(memory_space=pltpu.VMEM)
SM = pl.BlockSpec(memory_space=pltpu.SMEM)


def cosines(freq, place):
    phase = ((2 * place + 1) * freq) & 255
    scale = jnp.where(freq == 0, np.float32(np.sqrt(1 / 64)), np.float32(np.sqrt(2 / 64)))
    return scale * jnp.cos(phase.astype(f32) * np.float32(np.pi / 128))


def lines(shape, axis):
    return lax.broadcasted_iota(i32, shape, axis)


def spectrum():
    shape = (64, 128)
    return cosines(lines(shape, 0), lines(shape, 1) & 63)


def left_table(table):
    groups = [table[8 * ub : 8 * ub + 8] for ub in range(8) for _ in range(2)]
    shape = (128, 128)
    return jnp.where((lines(shape, 0) >> 3) & 1 == lines(shape, 1) >> 6, jnp.concatenate(groups, 0), 0.0)


def left_table_t():
    shape = (64, 128)
    r = lines(shape, 1)
    part = cosines((r >> 4) * 8 + (r & 7), lines(shape, 0))
    odd = (r >> 3) & 1
    return jnp.concatenate([jnp.where(odd == 0, part, 0.0), jnp.where(odd == 1, part, 0.0)], 0)


def right_table():
    shape = (64, COLS)
    j = lines(shape, 1)
    part = cosines((j >> 6) * 8 + (j & 7), lines(shape, 0))
    tile = (j >> 3) & 7
    return jnp.concatenate([jnp.where(tile == b, part, 0.0).astype(bf16) for b in range(8)], 0)


def right_table_t():
    table = spectrum()
    low = lines(table.shape, 1) < 64
    masked = jnp.where(low, table, 0.0), jnp.where(low, 0.0, table)
    zeros = jnp.zeros((8, 128), f32)
    columns = []
    for c in range(4):
        groups = [masked[b & 1][8 * vb : 8 * vb + 8] if b >> 1 == c else zeros for vb in range(8) for b in range(8)]
        columns.append(jnp.concatenate(groups, 0))
    return jnp.concatenate(columns, 1)


def dot(a, b):
    return jnp.dot(a, b, preferred_element_type=f32)


def split(x):
    high = x.astype(bf16)
    return high, (x - high.astype(f32)).astype(bf16)


def by_halves(run, x):
    return jnp.concatenate([run(x[:128]), run(x[128:])], 0)


def left_dot(table, x):
    high, low = split(x)
    return dot(table[0], high) + (dot(table[0], low) + dot(table[1], high))


def right_dot(x, table):
    high, low = split(x)
    return dot(high, table[0]) + (dot(low, table[0]) + dot(high, table[1]))


def low_lanes():
    return lax.broadcasted_iota(i32, (128, 128), 1) < 64


def to_slabs(grid, put):
    low = low_lanes()
    for q in range(4):
        top = grid[:128, 128 * q : 128 * (q + 1)]
        bottom = grid[128:, 128 * q : 128 * (q + 1)]
        even = jnp.where(low, top, pltpu.roll(bottom, 64, 1))
        odd = jnp.where(low, pltpu.roll(top, 64, 1), bottom)
        for ub in range(8):
            put(ub * 8 + 2 * q, even[16 * ub : 16 * (ub + 1)])
            put(ub * 8 + 2 * q + 1, odd[16 * ub : 16 * (ub + 1)])


def from_slabs(get):
    low = low_lanes()
    tops, bottoms = [], []
    for q in range(4):
        even = jnp.concatenate([get(ub * 8 + 2 * q) for ub in range(8)], 0)
        odd = jnp.concatenate([get(ub * 8 + 2 * q + 1) for ub in range(8)], 0)
        tops.append(jnp.where(low, even, pltpu.roll(odd, 64, 1)))
        bottoms.append(jnp.where(low, pltpu.roll(even, 64, 1), odd))
    return jnp.concatenate([jnp.concatenate(tops, 1), jnp.concatenate(bottoms, 1)], 0)


def list_all(kept, room):
    room[...] = jnp.full((1, 128), -1, i32)
    room[:, :KEEP] = kept[...]
    named = room[...]
    shape = (SLABS, 128)
    s, lane = lines(shape, 0), lines(shape, 1)
    hits = jnp.where(s == named, 1.0, 0.0)
    free = jnp.broadcast_to(1.0 - jnp.max(hits, axis=1, keepdims=True), shape)
    shape = (SLABS, SLABS)
    below = jnp.where(lines(shape, 1) < lines(shape, 0), 1.0, 0.0)
    rank = dot(below.astype(bf16), free.astype(bf16))
    here = jnp.where((lane - KEEP).astype(f32) == rank, free, 0.0)
    rest = jnp.sum(here * s.astype(f32), axis=0, keepdims=True)
    row = jnp.where(lane[:1] < KEEP, named.astype(f32), rest)
    room[...] = row.astype(i32)
    return row


def find_way(distances, way):
    sizes = [sum((distances[k] > 1 << bit).astype(i32) for bit in range(TOP)) for k in range(2)]
    way[0] = jnp.where(sizes[1] == TOP, sizes[0], TOP + sizes[1])


def public_kernel(distances, kept, public, full, early, way, room, listed, sem):
    find_way(distances, way)
    row = list_all(kept, room)
    to_scalars = pltpu.make_async_copy(room, listed, sem.at[0])
    to_scalars.start()
    left, right = left_table(spectrum()).astype(bf16), right_table()
    grid = by_halves(lambda x: dot(left, x), dot(public[...], right).astype(bf16))

    def put(s, slab):
        full[s] = slab.astype(bf16)

    to_slabs(grid, put)
    early[LEFT] = jnp.broadcast_to(row, (16, 128)).astype(bf16)
    to_scalars.wait()
    for j in range(LEFT):
        early[j] = full[listed[0, KEEP + j]]


def spread_kernel(own, other, out, sems):
    copies = []
    for x in range(out.shape[0]):
        for k, part in enumerate((own, other)):
            copies.append(pltpu.make_async_copy(part, out.at[x, k], sems.at[2 * x + k]))
    for copy in copies:
        copy.start()
    for copy in copies:
        copy.wait()


def own_place():
    return lax.axis_index("tp") & 1


def grads_kernel(count, grads, weight, turned, weight_coeffs):
    place = own_place()
    right = right_table()
    part = grads.shape[0] // 4
    for k in range(4):
        y = dot(grads[k * part : (k + 1) * part], right)
        token = k * part + lines((part, COLS), 0)
        y = jnp.where(token < count[...], y, 0.0).astype(bf16)
        for z in range(2):
            to = k * part + ((z + place) & 1) * (part // 2)
            turned[pl.ds(pl.multiple_of(to, part // 2), part // 2), :] = y[part // 2 * z : part // 2 * (z + 1)]
    left = left_table(spectrum()).astype(bf16)
    weight_coeffs[...] = by_halves(lambda x: dot(left, x), dot(weight[...], right).astype(bf16))


def weights_kernel(kept_row, acts, turned, weight_coeffs, public_full, packed, full, kept_coeffs, moved, slabs, kept, sem):
    to_scalars = pltpu.make_async_copy(kept_row, kept, sem.at[0])
    to_scalars.start()
    left = split(left_table(spectrum()))
    dims = (((1,), (1,)), ((), ()))
    x = acts[...].reshape(-1, ROWS)
    rows = []
    for h in range(2):
        half = x[:, 128 * h : 128 * (h + 1)]
        row = lax.dot_general(left[0], half, dims, preferred_element_type=f32)
        rows.append((row + lax.dot_general(left[1], half, dims, preferred_element_type=f32)).astype(bf16))
    change = -learn_rate * dot(jnp.concatenate(rows, 0), turned[...])
    moved[...] = change

    def put(s, slab):
        slabs[s] = slab

    to_slabs(weight_coeffs[...] + change, put)
    full[...] = public_full[...]
    to_scalars.wait()
    for i in range(KEEP):
        s = kept[0, i]
        slab = slabs[s]
        short = slab.astype(bf16)
        kept_coeffs[i] = slab
        packed[i] = short
        full[s] = short


def fill_kernel(listed, early, peer):
    for j in range(LEFT):
        peer[listed[KEEP + j]] = early[j]
    for i in range(KEEP):
        peer[listed[i]] = jnp.zeros((16, 128), bf16)


def mix(kept, peer, kept_coeffs, next_coeffs, put):
    for i in range(KEEP):
        s = kept[i]
        value = kept_coeffs[i]
        value = value + step * (peer[s].astype(f32) - value)
        next_coeffs[i] = value
        put(i, s, value.astype(bf16))


def mix_packed(kept, peer, kept_coeffs, packed, next_coeffs):
    def put(i, s, slab):
        packed[i] = slab

    mix(kept, peer, kept_coeffs, next_coeffs, put)


def near_kernel(kept, peer, kept_coeffs, packed, next_coeffs):
    mix_packed(kept, peer, kept_coeffs, packed, next_coeffs)


def unpack(listed, arrived, filled, peer):
    peer[...] = filled[...]
    for i in range(KEEP):
        peer[listed[i]] = arrived[i]


def far_packed_kernel(kept, listed, arrived, filled, kept_coeffs, packed, next_coeffs, peer):
    unpack(listed, arrived, filled, peer)
    mix_packed(kept, peer, kept_coeffs, packed, next_coeffs)


def far_full_kernel(kept, listed, arrived, filled, own, kept_coeffs, full, next_coeffs, peer):
    unpack(listed, arrived, filled, peer)
    full[...] = own[...]

    def put(i, s, slab):
        full[s] = slab

    mix(kept, peer, kept_coeffs, next_coeffs, put)


def base_kernel(kept, peer, public_full, kept_coeffs, next_coeffs, moved, weight, out, left_high, right_high, delta):
    delta[...] = step * peer[...].astype(f32) - 2 * step * public_full[...].astype(f32)
    for i in range(KEEP):
        s = kept[i]
        delta[s] = step * (peer[s].astype(f32) - kept_coeffs[i] - next_coeffs[i])
    grid = from_slabs(lambda s: delta[s]) + moved[...]
    left, right = split(left_table_t()), split(right_table_t())
    left_high[...] = left[0]
    right_high[...] = right[0]
    out[...] = weight[...].astype(f32) + by_halves(lambda x: left_dot(left, x), right_dot(grid, right))


def finish(get, base, left_t, right_t, out):
    grid = (step * from_slabs(lambda s: get(s).astype(f32))).astype(bf16)
    turned = dot(grid, right_t[...]).astype(bf16)
    out[...] = (base[...] + by_halves(lambda x: dot(left_t[...], x), turned)).astype(bf16)


def near_last_kernel(peer, base, left_t, right_t, out):
    finish(lambda s: peer[s], base, left_t, right_t, out)


def far_last_kernel(listed, arrived, filled, base, left_t, right_t, out, slabs):
    unpack(listed, arrived, filled, slabs)
    finish(lambda s: slabs[s], base, left_t, right_t, out)


def call(kernel, outs, specs, scratch=(), flops=0, moves=0, out_specs=None):
    return pl.pallas_call(
        kernel,
        out_shape=[jax.ShapeDtypeStruct(shape, kind) for shape, kind in outs],
        in_specs=specs,
        out_specs=out_specs or [VM] * len(outs),
        scratch_shapes=list(scratch),
        compiler_params=pltpu.CompilerParams(vmem_limit_bytes=16 * 2**20),
        cost_estimate=pl.CostEstimate(flops=flops, bytes_accessed=moves, transcendentals=0),
    )


SLAB16 = ((SLABS, 16, 128), bf16)
KEPT32 = ((KEEP, 16, 128), f32)
KEPT16 = ((KEEP, 16, 128), bf16)
GRID32 = ((ROWS, COLS), f32)
GRID16 = ((ROWS, COLS), bf16)
REST = pltpu.SMEM((SLABS + 1,), i32)
ROOM32, ROOM16 = pltpu.VMEM((SLABS, 16, 128), f32), pltpu.VMEM((SLABS, 16, 128), bf16)


ANY = pl.BlockSpec(memory_space=pl.ANY)


def sems(count):
    return pltpu.SemaphoreType.DMA((count,))


def do_public(distances, kept, public):
    outs = [SLAB16, ((LEFT + 1, 16, 128), bf16), ((1,), i32)]
    scratch = [pltpu.VMEM((1, 128), i32), pltpu.SMEM((1, 128), i32), sems(1)]
    return call(public_kernel, outs, [SM, VM, VM], scratch, 10**9, 2**21, [VM, VM, SM])(distances, kept, public)


def do_spread(count, own, other):
    outs = [((count, 2) + own.shape, bf16)]
    return call(spread_kernel, outs, [VM, VM], [sems(2 * count)], 10**5, 2**20, [ANY])(own, other)[0]


def do_grads(count, grads, weight):
    return call(grads_kernel, [(grads.shape, bf16), GRID32], [VM] * 3, (), 2 * 10**9, 2**22)(count, grads, weight)


def do_weights(kept, *rest):
    outs = [KEPT16, SLAB16, KEPT32, GRID32]
    return call(weights_kernel, outs, [VM] * 5, [ROOM32, pltpu.SMEM((1, KEEP), i32), sems(1)], 3 * 10**8, 2**21)(kept, *rest)


def do_fill(listed, early):
    return call(fill_kernel, [SLAB16], [SM, VM], (), 10**6, 2**18)(listed, early)[0]


def do_near(kept, peer, kept_coeffs):
    return call(near_kernel, [KEPT16, KEPT32], [SM] + [VM] * 2, (), 10**6, 2**19)(kept, peer, kept_coeffs)


def do_far_packed(kept, listed, *rest):
    return call(far_packed_kernel, [KEPT16, KEPT32, SLAB16], [SM, SM] + [VM] * 3, (), 10**6, 2**19)(kept, listed, *rest)


def do_far_full(kept, listed, *rest):
    return call(far_full_kernel, [SLAB16, KEPT32, SLAB16], [SM, SM] + [VM] * 4, (), 10**6, 2**19)(kept, listed, *rest)


def do_base(kept, *rest):
    outs = [GRID32, ((128, 128), bf16), ((COLS, COLS), bf16)]
    return call(base_kernel, outs, [SM] + [VM] * 6, [ROOM32], 10**9, 2**22)(kept, *rest)


def do_near_last(*args):
    return call(near_last_kernel, [GRID16], [VM] * 4, (), 2 * 10**8, 2**20)(*args)[0]


def do_far_last(listed, *rest):
    return call(far_last_kernel, [GRID16], [SM] + [VM] * 5, [ROOM16], 2 * 10**8, 2**20)(listed, *rest)[0]


def swapped(block, axis, bit):
    count = lax.axis_size(axis)
    return lax.ppermute(block, axis, [(i, i ^ (1 << bit)) for i in range(count)])


def peers_list(early):
    return early[LEFT, 0, :SLABS].astype(i32)


def shards(activations, out_grads, weight, public, counts, kept, distances):
    count_x = lax.axis_size("tp") // 2
    groups = [[2 * x + z for x in range(count_x)] for z in range(2)]
    acts, grads, weight, public, kept = activations[0], out_grads[0], weight[0], public[0], kept[0, 0]

    other = swapped(acts, "tp", 0)
    public_full, early, way = do_public(distances, kept[None], public)
    early_far = swapped(early, "rep", TOP)
    other, early = lax.optimization_barrier((other, early))
    pairs = do_spread(count_x, acts, other)
    pairs, counts = lax.optimization_barrier((pairs, counts[:, None]))
    rows = lax.all_to_all(pairs, "tp", 0, 0, axis_index_groups=groups)
    turned, weight_coeffs = do_grads(counts, grads, weight)
    packed, full, kept_coeffs, moved = do_weights(kept[None], rows, turned, weight_coeffs, public_full)

    def rounds(first, second):
        def run(packed, full, early, early_far):
            if first == TOP:
                arrived = swapped(packed, "rep", first)
                if second in PACKED:
                    early, packed = lax.optimization_barrier((early, packed))
                    early_second = swapped(early, "rep", second)
                listed = peers_list(early_far)
                filled = do_fill(listed, early_far)
                if second in PACKED:
                    late, next_coeffs, peer = do_far_packed(kept, listed, arrived, filled, kept_coeffs)
                else:
                    late, next_coeffs, peer = do_far_full(kept, listed, arrived, filled, full, kept_coeffs)
            else:
                early_second = early_far
                peer = swapped(full, "rep", first)
                late, next_coeffs = do_near(kept, peer, kept_coeffs)
            arrived = swapped(late, "rep", second)
            last = do_base(kept, peer, public_full, kept_coeffs, next_coeffs, moved, weight)
            if second in PACKED:
                listed = peers_list(early_second)
                return do_far_last(listed, arrived, do_fill(listed, early_second), *last)
            return do_near_last(arrived, *last)

        return run

    ways = [(bit, TOP) for bit in range(TOP)] + [(TOP, bit) for bit in range(TOP)]
    return lax.switch(way[0], [rounds(*pair) for pair in ways], packed, full, early, early_far)[None]


def solution(mesh):
    return jax.shard_map(
        shards,
        mesh=mesh,
        in_specs=(
            P("rep", "tp", None),
            P("rep", None, "tp"),
            P("rep", None, "tp"),
            P("rep", None, "tp"),
            P("rep"),
            P("rep", "tp", None),
            P(),
        ),
        out_specs=P("rep", None, "tp"),
        check_vma=False,
    )
```

profile of v0, /device:TPU:34, one launch (start us, length us, event | category | flops | bytes accessed | tf_op | source)
XLA Modules:
  0.0 60.2 jit_solution(349959335755081067)
XLA Ops:
  0.0 10.9 %collective-permute-start.23 = (bf16[128,256]{1,0:T(8,128)(2,1)}, bf16[128,256]{1,0:T(8,128)(2,1)S(1)}, u32[]{:S(2)}, u32[]{:S(2)}) collective-permute-start(bf16[128,256]{1,0:T(8,128)(2,1)} %bitcast.59), channel_id=1, source_target_pairs={{0,1},{1,0},{2,3},{3,2},{4,5},{5,4},{6,7},{7,6},{8,9},{9,8},{10,11... | collective-permute-start | bytes 196616 | tf_op jit(solution)/shard_map/ppermute | solution.py:373
  10.9 0.0 copy-start.3
  10.9 0.0 copy-start.5
  10.9 0.6 %copy-done.3 = s32[2]{0:T(128)S(1)} copy-done((s32[2]{0:T(128)S(1)}, s32[2]{0:T(128)}, u32[]{:S(2)}) %copy-start.3) | copy-done | bytes 32
  11.6 0.0 copy-done.5
  11.6 0.0 copy-start.2
  11.6 0.9 %copy-done.2 = bf16[1,256,512]{2,1,0:T(8,128)(2,1)S(1)} copy-done((bf16[1,256,512]{2,1,0:T(8,128)(2,1)S(1)}, bf16[1,256,512]{2,1,0:T(8,128)(2,1)}, u32[]{:S(2)}) %copy-start.2) | copy-done | bytes 262168
  12.5 2.3 %shard_map.83 = (bf16[64,16,128]{2,1,0:T(8,128)(2,1)S(1)}, bf16[25,16,128]{2,1,0:T(8,128)(2,1)}, s32[1]{0:T(128)}) custom-call(s32[2]{0:T(128)S(1)} %copy-done.3, s32[1,40]{1,0:T(1,128)S(1)} %bitcast.73, bf16[256,512]{1,0:T(8,128)(2,1)S(1)} %bitcast.62), custom_call_target="tpu_custom_call" | custom-call | flops 1000000000 | bytes 2097152 | tf_op jit(solution)/shard_map/pallas_call | solution.py:325
  14.9 0.0 copy-start.1
  14.9 0.0 collective-permute-done.23.other
  14.9 0.0 copy-done
  14.9 0.9 %shard_map.84 = bf16[4,2,128,256]{3,2,1,0:T(8,128)(2,1)} custom-call(bf16[128,256]{1,0:T(8,128)(2,1)S(1)} %bitcast.60, bf16[128,256]{1,0:T(8,128)(2,1)S(1)} %collective-permute-done.23.other), custom_call_target="tpu_custom_call" | custom-call | flops 100000 | bytes 1048576 | tf_op jit(solution)/shard_map/pallas_call | solution.py:330
  15.8 4.8 %all-to-all-start = ((bf16[4,2,128,256]{3,2,1,0:T(8,128)(2,1)}), bf16[4,2,128,256]{3,2,1,0:T(8,128)(2,1)S(1)}, u32[]{:S(2)}, u32[]{:S(2)}) async-start(bf16[4,2,128,256]{3,2,1,0:T(8,128)(2,1)} %shard_map.84), calls=%async_computation | async-start | bytes 1048576 | tf_op jit(solution)/shard_map/all_to_all | solution.py:391
  20.6 4.3 %collective-permute-start.22 = (bf16[25,16,128]{2,1,0:T(8,128)(2,1)}, bf16[25,16,128]{2,1,0:T(8,128)(2,1)S(1)}, u32[]{:S(2)}, u32[]{:S(2)}) collective-permute-start(bf16[25,16,128]{2,1,0:T(8,128)(2,1)} %get-tuple-element.324), channel_id=1, source_target_pairs={{0,256},{8,264},{16,272},{24,280},{32,288},{40,296},{48,304},{56,3... | collective-permute-start | bytes 307208 | tf_op jit(solution)/shard_map/ppermute | solution.py:373
  25.6 0.0 copy-done.1
  25.6 2.4 %shard_map.85 = (bf16[1024,512]{1,0:T(8,128)(2,1)S(1)}, f32[256,512]{1,0:T(8,128)S(1)}) custom-call(s32[1,1]{1,0:T(1,128)} %bitcast.58.count, bf16[1024,512]{1,0:T(8,128)(2,1)S(1)} %bitcast.61, bf16[256,512]{1,0:T(8,128)(2,1)} %bitcast.85), custom_call_target="tpu_custom_call" | custom-call | flops 2000000000 | bytes 4194304 | tf_op jit(solution)/shard_map/pallas_call | solution.py:334
  28.7 0.0 all-to-all-done.acts
  28.7 0.0 copy-start.6
  28.7 1.1 %shard_map.86 = (bf16[40,16,128]{2,1,0:T(8,128)(2,1)S(1)}, bf16[64,16,128]{2,1,0:T(8,128)(2,1)S(1)}, f32[40,16,128]{2,1,0:T(8,128)S(1)}, f32[256,512]{1,0:T(8,128)S(1)}) custom-call(s32[1,40]{1,0:T(1,128)S(1)} %bitcast.74, bf16[4,2,128,256]{3,2,1,0:T(8,128)(2,1)S(1)} %all-to-all-done.acts, bf16[1024,512]{1,0:T(8,128)(2,1)S(1)} %get-tuple-element.317.turned, ...), custom_call_target="tpu_custom_call" | custom-call | flops 300000000 | bytes 2097152 | tf_op jit(solution)/shard_map/pallas_call | solution.py:339
  29.7 0.0 collective-permute-done.22
  29.8 0.0 copy-done.6
  29.8 29.7 %conditional.1 = (bf16[1,256,512]{2,1,0:T(8,128)(2,1)S(1)}) conditional(s32[]{:T(128)} %bitcast.36, (bf16[25,16,128]{2,1,0:T(8,128)(2,1)S(1)}, bf16[64,16,128]{2,1,0:T(8,128)(2,1)S(1)}, s32[40]{0:T(128)S(1)}, f32[40,16,128]{2,1,0:T(8,128)S(1)}, bf16[64,16,128]{2,1,0:T(8,128)(2,1)S(1)}, ...), branch_computations={%region_0.0_spmd, %region_1.0_spmd, %region_2.0_spmd, %region_3.0_... | conditional | flops 1203000064 | bytes 8012672 | solution.py:422
  29.8 2.7 %collective-permute-start.4 = (bf16[64,16,128]{2,1,0:T(8,128)(2,1)S(1)}, bf16[64,16,128]{2,1,0:T(8,128)(2,1)S(1)}, u32[]{:S(2)}, u32[]{:S(2)}) collective-permute-start(bf16[64,16,128]{2,1,0:T(8,128)(2,1)S(1)} %get-tuple-element.193), channel_id=1, source_target_pairs={{0,32},{8,40},{16,48},{24,56},{32,0},{40,8},{48,16},{56,24},{64,96... | collective-permute-start | bytes 786440 | tf_op jit(solution)/shard_map/cond/branch_2_fun/ppermute | solution.py:373
  32.5 12.7 %collective-permute-done.4.peer = bf16[64,16,128]{2,1,0:T(8,128)(2,1)S(1)} collective-permute-done((bf16[64,16,128]{2,1,0:T(8,128)(2,1)S(1)}, bf16[64,16,128]{2,1,0:T(8,128)(2,1)S(1)}, u32[]{:S(2)}, u32[]{:S(2)}) %collective-permute-start.4) | collective-permute-done | bytes 262176 | tf_op jit(solution)/shard_map/cond/branch_2_fun/ppermute | solution.py:373
  45.2 0.6 branch_2_fun.4
  45.8 3.4 %collective-permute-start.5 = (bf16[40,16,128]{2,1,0:T(8,128)(2,1)S(1)}, bf16[40,16,128]{2,1,0:T(8,128)(2,1)S(1)}, u32[]{:S(2)}, u32[]{:S(2)}) collective-permute-start(bf16[40,16,128]{2,1,0:T(8,128)(2,1)S(1)} %get-tuple-element.195), channel_id=1, source_target_pairs={{0,256},{8,264},{16,272},{24,280},{32,288},{40,296},{48,304},{56,3... | collective-permute-start | bytes 491528 | tf_op jit(solution)/shard_map/cond/branch_2_fun/ppermute | solution.py:373
  49.3 0.6 branch_2_fun.5.filled
  49.9 1.8 %branch_2_fun.6 = (f32[256,512]{1,0:T(8,128)S(1)}, bf16[128,128]{1,0:T(8,128)(2,1)S(1)}, bf16[512,512]{1,0:T(8,128)(2,1)S(1)}) custom-call(s32[40]{0:T(128)S(1)} %get-tuple-element.192.kept, bf16[64,16,128]{2,1,0:T(8,128)(2,1)S(1)} %collective-permute-done.4.peer, bf16[64,16,128]{2,1,0:T(8,128)(2,1)S(1)} %get-tuple-element.196.public_full, ...), custom_call_target="tpu_custom_call" | custom-call | flops 1000000000 | bytes 4194304 | tf_op jit(solution)/shard_map/cond/branch_2_fun/pallas_call | solution.py:360
  51.7 6.4 %collective-permute-done.5.arrived = bf16[40,16,128]{2,1,0:T(8,128)(2,1)S(1)} collective-permute-done((bf16[40,16,128]{2,1,0:T(8,128)(2,1)S(1)}, bf16[40,16,128]{2,1,0:T(8,128)(2,1)S(1)}, u32[]{:S(2)}, u32[]{:S(2)}) %collective-permute-start.5) | collective-permute-done | bytes 163872 | tf_op jit(solution)/shard_map/cond/branch_2_fun/ppermute | solution.py:373
  58.1 1.1 %branch_2_fun.7 = bf16[256,512]{1,0:T(8,128)(2,1)S(1)} custom-call(s32[64]{0:T(128)S(1)} %bitcast_convert_fusion.2.listed, bf16[40,16,128]{2,1,0:T(8,128)(2,1)S(1)} %collective-permute-done.5.arrived, bf16[64,16,128]{2,1,0:T(8,128)(2,1)S(1)} %branch_2_fun.5.filled, f32[256,512]{1,0:T(8,128)S(1)} %get-tuple-element.200.base, ...), custom_call_target="tpu_custom_call" | custom-call | flops 200000000 | bytes 1048576 | tf_op jit(solution)/shard_map/cond/branch_2_fun/pallas_call | solution.py:368
  59.5 0.0 copy-start.4
  59.5 0.7 %copy-done.4 = bf16[1,256,512]{2,1,0:T(8,128)(2,1)} copy-done((bf16[1,256,512]{2,1,0:T(8,128)(2,1)}, bf16[1,256,512]{2,1,0:T(8,128)(2,1)S(1)}, u32[]{:S(2)}) %copy-start.4) | copy-done | bytes 262168
  (2 shorter events, 0.0 us)
Async XLA Ops:
  0.0 14.9 %collective-permute-start.23 = (bf16[128,256]{1,0:T(8,128)(2,1)}, bf16[128,256]{1,0:T(8,128)(2,1)S(1)}, u32[]{:S(2)}, u32[]{:S(2)}) collective-permute-start(bf16[128,256]{1,0:T(8,128)(2,1)} %bitcast.59), channel_id=1, source_target_pairs={{0,1},{1,0},{2,3},{3,2},{4,5},{5,4},{6,7},{7,6},{8,9},{9,8},{10,11... | collective-permute-start | bytes 196616 | tf_op jit(solution)/shard_map/ppermute | solution.py:373
  10.9 0.7 %copy-start.3 = (s32[2]{0:T(128)S(1)}, s32[2]{0:T(128)}, u32[]{:S(2)}) copy-start(s32[2]{0:T(128)} %distances.1) | copy-start | bytes 28
  10.9 0.7 %copy-start.5 = (s32[1,1,40]{2,1,0:T(1,128)S(1)}, s32[1,1,40]{2,1,0:T(1,128)}, u32[]{:S(2)}) copy-start(s32[1,1,40]{2,1,0:T(1,128)} %param.22) | copy-start | bytes 484
  11.6 0.9 %copy-start.2 = (bf16[1,256,512]{2,1,0:T(8,128)(2,1)S(1)}, bf16[1,256,512]{2,1,0:T(8,128)(2,1)}, u32[]{:S(2)}) copy-start(bf16[1,256,512]{2,1,0:T(8,128)(2,1)} %param.20) | copy-start | bytes 786436
  12.5 2.4 %copy-start = (bf16[1,128,256]{2,1,0:T(8,128)(2,1)S(1)}, bf16[1,128,256]{2,1,0:T(8,128)(2,1)}, u32[]{:S(2)}) copy-start(bf16[1,128,256]{2,1,0:T(8,128)(2,1)} %param.17) | copy-start | bytes 196612
  14.9 10.7 %copy-start.1 = (bf16[1,1024,512]{2,1,0:T(8,128)(2,1)S(1)}, bf16[1,1024,512]{2,1,0:T(8,128)(2,1)}, u32[]{:S(2)}) copy-start(bf16[1,1024,512]{2,1,0:T(8,128)(2,1)} %param.18) | copy-start | bytes 3145732
  15.8 12.9 %all-to-all-start = ((bf16[4,2,128,256]{3,2,1,0:T(8,128)(2,1)}), bf16[4,2,128,256]{3,2,1,0:T(8,128)(2,1)S(1)}, u32[]{:S(2)}, u32[]{:S(2)}) async-start(bf16[4,2,128,256]{3,2,1,0:T(8,128)(2,1)} %shard_map.84), calls=%async_computation | async-start | bytes 1048576 | tf_op jit(solution)/shard_map/all_to_all | solution.py:391
  20.6 9.1 %collective-permute-start.22 = (bf16[25,16,128]{2,1,0:T(8,128)(2,1)}, bf16[25,16,128]{2,1,0:T(8,128)(2,1)S(1)}, u32[]{:S(2)}, u32[]{:S(2)}) collective-permute-start(bf16[25,16,128]{2,1,0:T(8,128)(2,1)} %get-tuple-element.324), channel_id=1, source_target_pairs={{0,256},{8,264},{16,272},{24,280},{32,288},{40,296},{48,304},{56,3... | collective-permute-start | bytes 307208 | tf_op jit(solution)/shard_map/ppermute | solution.py:373
  28.7 1.1 %copy-start.6 = (bf16[1,256,512]{2,1,0:T(8,128)(2,1)S(1)}, bf16[1,256,512]{2,1,0:T(8,128)(2,1)}, u32[]{:S(2)}) copy-start(bf16[1,256,512]{2,1,0:T(8,128)(2,1)} %param.19) | copy-start | bytes 786436
  29.8 15.4 %collective-permute-start.4 = (bf16[64,16,128]{2,1,0:T(8,128)(2,1)S(1)}, bf16[64,16,128]{2,1,0:T(8,128)(2,1)S(1)}, u32[]{:S(2)}, u32[]{:S(2)}) collective-permute-start(bf16[64,16,128]{2,1,0:T(8,128)(2,1)S(1)} %get-tuple-element.193), channel_id=1, source_target_pairs={{0,32},{8,40},{16,48},{24,56},{32,0},{40,8},{48,16},{56,24},{64,96... | collective-permute-start | bytes 786440 | tf_op jit(solution)/shard_map/cond/branch_2_fun/ppermute | solution.py:373
  45.8 12.3 %collective-permute-start.5 = (bf16[40,16,128]{2,1,0:T(8,128)(2,1)S(1)}, bf16[40,16,128]{2,1,0:T(8,128)(2,1)S(1)}, u32[]{:S(2)}, u32[]{:S(2)}) collective-permute-start(bf16[40,16,128]{2,1,0:T(8,128)(2,1)S(1)} %get-tuple-element.195), channel_id=1, source_target_pairs={{0,256},{8,264},{16,272},{24,280},{32,288},{40,296},{48,304},{56,3... | collective-permute-start | bytes 491528 | tf_op jit(solution)/shard_map/cond/branch_2_fun/ppermute | solution.py:373
  59.5 0.7 %copy-start.4 = (bf16[1,256,512]{2,1,0:T(8,128)(2,1)}, bf16[1,256,512]{2,1,0:T(8,128)(2,1)S(1)}, u32[]{:S(2)}) copy-start(bf16[1,256,512]{2,1,0:T(8,128)(2,1)S(1)} %get-tuple-element.377) | copy-start | bytes 786436
where the time goes:
time: 60.5 us; the launch traced here: 60.2 us
  starting transfers between devices  26.1 us (43%)
  waiting for transfers between devices  19.2 us (32%)
  Pallas kernels  10.8 us (18%)
  local copies, waits for them, and re-layouts  2.32 us (4%)
  between operations  1.43 us (2%)
    ppermute x4, starting transfers between devices, swapped(): return lax.ppermute(block, axis, [(i, i ^ 1 << bit) for i in range(count)])  21.3 us
    ppermute x4, waiting for transfers between devices, swapped(): return lax.ppermute(block, axis, [(i, i ^ 1 << bit) for i in range(count)])  19.2 us
    all_to_all x1, starting transfers between devices, shards(): rows = lax.all_to_all(pairs, 'tp', 0, 0, axis_index_groups=groups)  4.84 us
    pallas_call x1, Pallas kernels, do_grads(): call(grads_kernel, [(grads.shape, bf16), GRID32], [VM] * 3, (), 2 * 10 **...  2.44 us
    pallas_call x1, Pallas kernels, do_public(): call(public_kernel, outs, [SM, VM, VM], scratch, 10 ** 9, 2 ** 21, [VM, V...  2.33 us
    unnamed x14, local copies, waits for them, and re-layouts  2.32 us
    pallas_call x1, Pallas kernels, do_base(): call(base_kernel, outs, [SM] + [VM] * 6, [ROOM32], 10 ** 9, 2 ** 22)  1.84 us
  transfers between devices with their start and end apart: 5, of which 2 were waited for; matrix products, arithmetic and copies ran while one was open for 0% of the time, Pallas kernels for 14%

commit v1 on v0

--- a/solution.py
+++ b/solution.py
@@ -11,7 +11,7 @@
 step = 0.25
 ROWS, COLS, KEEP, SLABS, TOP = 256, 512, 40, 64, 5
 LEFT = SLABS - KEEP
-PACKED = (2, 3, TOP)
+PACKED = (1, 2, 3, 4, TOP)
 f32, bf16, i32 = jnp.float32, jnp.bfloat16, jnp.int32
 VM = pl.BlockSpec(memory_space=pltpu.VMEM)
 SM = pl.BlockSpec(memory_space=pltpu.SMEM)

time: 60.5 us -> 52.1 us (0.86)
  the two profiles are of different devices: /device:TPU:34 before, /device:TPU:10 now
where the time goes in v1:
time: 52.1 us; the launch traced here: 51.7 us
  starting transfers between devices  25.7 us (49%)
  waiting for transfers between devices  11 us (21%)
  Pallas kernels  10.8 us (21%)
  local copies, waits for them, and re-layouts  2.32 us (4%)
  between operations  1.49 us (3%)
    ppermute x4, starting transfers between devices, swapped(): return lax.ppermute(block, axis, [(i, i ^ 1 << bit) for i in range(count)])  20.9 us
    ppermute x4, waiting for transfers between devices, swapped(): return lax.ppermute(block, axis, [(i, i ^ 1 << bit) for i in range(count)])  11 us
    all_to_all x1, starting transfers between devices, shards(): rows = lax.all_to_all(pairs, 'tp', 0, 0, axis_index_groups=groups)  4.84 us
    pallas_call x1, Pallas kernels, do_grads(): call(grads_kernel, [(grads.shape, bf16), GRID32], [VM] * 3, (), 2 * 10 **...  2.44 us
    pallas_call x1, Pallas kernels, do_public(): call(public_kernel, outs, [SM, VM, VM], scratch, 10 ** 9, 2 ** 21, [VM, V...  2.33 us
    unnamed x14, local copies, waits for them, and re-layouts  2.32 us
    pallas_call x1, Pallas kernels, do_base(): call(base_kernel, outs, [SM] + [VM] * 6, [ROOM32], 10 ** 9, 2 ** 22)  1.82 us
    pallas_call x1, Pallas kernels, do_far_last(): call(far_last_kernel, [GRID16], [SM] + [VM] * 5, [ROOM16], 2 * 10 ** 8, 2...  1.1 us
  transfers between devices with their start and end apart: 5, of which 2 were waited for; matrix products, arithmetic and copies ran while one was open for 0% of the time, Pallas kernels for 16%

profile of v1, /device:TPU:10, one launch (start us, length us, event | category | flops | bytes accessed | tf_op | source)
XLA Modules:
  0.0 51.7 jit_solution(9814242681981823124)
XLA Ops:
  0.0 10.9 %collective-permute-start.25 = (bf16[128,256]{1,0:T(8,128)(2,1)}, bf16[128,256]{1,0:T(8,128)(2,1)S(1)}, u32[]{:S(2)}, u32[]{:S(2)}) collective-permute-start(bf16[128,256]{1,0:T(8,128)(2,1)} %bitcast.69), channel_id=1, source_target_pairs={{0,1},{1,0},{2,3},{3,2},{4,5},{5,4},{6,7},{7,6},{8,9},{9,8},{10,11... | collective-permute-start | bytes 196616 | tf_op jit(solution)/shard_map/ppermute | solution.py:373
  10.9 0.0 copy-start.3
  10.9 0.0 copy-start.5
  10.9 0.6 %copy-done.3 = s32[2]{0:T(128)S(1)} copy-done((s32[2]{0:T(128)S(1)}, s32[2]{0:T(128)}, u32[]{:S(2)}) %copy-start.3) | copy-done | bytes 32
  11.6 0.0 copy-done.5
  11.6 0.9 %copy-done.2 = bf16[1,256,512]{2,1,0:T(8,128)(2,1)S(1)} copy-done((bf16[1,256,512]{2,1,0:T(8,128)(2,1)S(1)}, bf16[1,256,512]{2,1,0:T(8,128)(2,1)}, u32[]{:S(2)}) %copy-start.2) | copy-done | bytes 262168
  12.5 0.0 copy-start
  12.5 2.3 %shard_map.83 = (bf16[64,16,128]{2,1,0:T(8,128)(2,1)S(1)}, bf16[25,16,128]{2,1,0:T(8,128)(2,1)}, s32[1]{0:T(128)}) custom-call(s32[2]{0:T(128)S(1)} %copy-done.3, s32[1,40]{1,0:T(1,128)S(1)} %bitcast.83, bf16[256,512]{1,0:T(8,128)(2,1)S(1)} %bitcast.72), custom_call_target="tpu_custom_call" | custom-call | flops 1000000000 | bytes 2097152 | tf_op jit(solution)/shard_map/pallas_call | solution.py:325
  14.9 0.0 copy-start.1
  14.9 0.0 collective-permute-done.25.other
  14.9 0.0 copy-done
  14.9 0.9 %shard_map.84 = bf16[4,2,128,256]{3,2,1,0:T(8,128)(2,1)} custom-call(bf16[128,256]{1,0:T(8,128)(2,1)S(1)} %bitcast.70, bf16[128,256]{1,0:T(8,128)(2,1)S(1)} %collective-permute-done.25.other), custom_call_target="tpu_custom_call" | custom-call | flops 100000 | bytes 1048576 | tf_op jit(solution)/shard_map/pallas_call | solution.py:330
  15.8 4.8 %all-to-all-start = ((bf16[4,2,128,256]{3,2,1,0:T(8,128)(2,1)}), bf16[4,2,128,256]{3,2,1,0:T(8,128)(2,1)S(1)}, u32[]{:S(2)}, u32[]{:S(2)}) async-start(bf16[4,2,128,256]{3,2,1,0:T(8,128)(2,1)} %shard_map.84), calls=%async_computation | async-start | bytes 1048576 | tf_op jit(solution)/shard_map/all_to_all | solution.py:391
  20.6 4.3 %collective-permute-start.24 = (bf16[25,16,128]{2,1,0:T(8,128)(2,1)}, bf16[25,16,128]{2,1,0:T(8,128)(2,1)S(1)}, u32[]{:S(2)}, u32[]{:S(2)}) collective-permute-start(bf16[25,16,128]{2,1,0:T(8,128)(2,1)} %get-tuple-element.326), channel_id=1, source_target_pairs={{0,256},{8,264},{16,272},{24,280},{32,288},{40,296},{48,304},{56,3... | collective-permute-start | bytes 307208 | tf_op jit(solution)/shard_map/ppermute | solution.py:373
  25.6 0.0 copy-done.1
  25.6 2.4 %shard_map.85 = (bf16[1024,512]{1,0:T(8,128)(2,1)S(1)}, f32[256,512]{1,0:T(8,128)S(1)}) custom-call(s32[1,1]{1,0:T(1,128)} %bitcast.68.count, bf16[1024,512]{1,0:T(8,128)(2,1)S(1)} %bitcast.71, bf16[256,512]{1,0:T(8,128)(2,1)} %bitcast.95), custom_call_target="tpu_custom_call" | custom-call | flops 2000000000 | bytes 4194304 | tf_op jit(solution)/shard_map/pallas_call | solution.py:334
  28.7 0.0 all-to-all-done.acts
  28.7 0.0 copy-start.6
  28.7 1.1 %shard_map.86 = (bf16[40,16,128]{2,1,0:T(8,128)(2,1)S(1)}, bf16[64,16,128]{2,1,0:T(8,128)(2,1)S(1)}, f32[40,16,128]{2,1,0:T(8,128)S(1)}, f32[256,512]{1,0:T(8,128)S(1)}) custom-call(s32[1,40]{1,0:T(1,128)S(1)} %bitcast.84, bf16[4,2,128,256]{3,2,1,0:T(8,128)(2,1)S(1)} %all-to-all-done.acts, bf16[1024,512]{1,0:T(8,128)(2,1)S(1)} %get-tuple-element.319.turned, ...), custom_call_target="tpu_custom_call" | custom-call | flops 300000000 | bytes 2097152 | tf_op jit(solution)/shard_map/pallas_call | solution.py:339
  29.8 0.0 collective-permute-done.24
  29.8 0.0 copy-done.6
  29.8 21.2 %conditional.1 = (bf16[1,256,512]{2,1,0:T(8,128)(2,1)S(1)}) conditional(s32[]{:T(128)} %bitcast.40, (bf16[25,16,128]{2,1,0:T(8,128)(2,1)S(1)}, bf16[64,16,128]{2,1,0:T(8,128)(2,1)S(1)}, s32[40]{0:T(128)S(1)}, f32[40,16,128]{2,1,0:T(8,128)S(1)}, bf16[64,16,128]{2,1,0:T(8,128)(2,1)S(1)}, ...), branch_computations={%region_0.0_spmd, %region_1.0_spmd, %region_2.0_spmd, %region_3.0_... | conditional | flops 1203000064 | bytes 8012672 | solution.py:422
  29.9 2.4 %collective-permute-start.2 = (bf16[64,16,128]{2,1,0:T(8,128)(2,1)S(1)}, bf16[64,16,128]{2,1,0:T(8,128)(2,1)S(1)}, u32[]{:S(2)}, u32[]{:S(2)}) collective-permute-start(bf16[64,16,128]{2,1,0:T(8,128)(2,1)S(1)} %get-tuple-element.181), channel_id=1, source_target_pairs={{0,16},{8,24},{16,0},{24,8},{32,48},{40,56},{48,32},{56,40},{64,80... | collective-permute-start | bytes 786440 | tf_op jit(solution)/shard_map/cond/branch_1_fun/ppermute | solution.py:373
  32.2 6.5 %collective-permute-done.2.peer = bf16[64,16,128]{2,1,0:T(8,128)(2,1)S(1)} collective-permute-done((bf16[64,16,128]{2,1,0:T(8,128)(2,1)S(1)}, bf16[64,16,128]{2,1,0:T(8,128)(2,1)S(1)}, u32[]{:S(2)}, u32[]{:S(2)}) %collective-permute-start.2) | collective-permute-done | bytes 262176 | tf_op jit(solution)/shard_map/cond/branch_1_fun/ppermute | solution.py:373
  38.8 0.6 %branch_1_fun.4 = (bf16[40,16,128]{2,1,0:T(8,128)(2,1)S(1)}, f32[40,16,128]{2,1,0:T(8,128)S(1)}) custom-call(s32[40]{0:T(128)S(1)} %get-tuple-element.180.kept, bf16[64,16,128]{2,1,0:T(8,128)(2,1)S(1)} %collective-permute-done.2.peer, f32[40,16,128]{2,1,0:T(8,128)S(1)} %get-tuple-element.182.kept_coeffs), custom_call_target="tpu_custom_call" | custom-call | flops 1000000 | bytes 524288 | tf_op jit(solution)/shard_map/cond/branch_1_fun/pallas_call | solution.py:347
  39.4 3.4 %collective-permute-start.3 = (bf16[40,16,128]{2,1,0:T(8,128)(2,1)S(1)}, bf16[40,16,128]{2,1,0:T(8,128)(2,1)S(1)}, u32[]{:S(2)}, u32[]{:S(2)}) collective-permute-start(bf16[40,16,128]{2,1,0:T(8,128)(2,1)S(1)} %get-tuple-element.183), channel_id=1, source_target_pairs={{0,256},{8,264},{16,272},{24,280},{32,288},{40,296},{48,304},{56,3... | collective-permute-start | bytes 491528 | tf_op jit(solution)/shard_map/cond/branch_1_fun/ppermute | solution.py:373
  42.8 0.6 %branch_1_fun.5.filled = bf16[64,16,128]{2,1,0:T(8,128)(2,1)S(1)} custom-call(s32[64]{0:T(128)S(1)} %bitcast_convert_fusion.1.listed, bf16[25,16,128]{2,1,0:T(8,128)(2,1)S(1)} %get-tuple-element.179.early), custom_call_target="tpu_custom_call" | custom-call | flops 1000000 | bytes 262144 | tf_op jit(solution)/shard_map/cond/branch_1_fun/pallas_call | solution.py:343
  43.4 1.8 %branch_1_fun.6 = (f32[256,512]{1,0:T(8,128)S(1)}, bf16[128,128]{1,0:T(8,128)(2,1)S(1)}, bf16[512,512]{1,0:T(8,128)(2,1)S(1)}) custom-call(s32[40]{0:T(128)S(1)} %get-tuple-element.180.kept, bf16[64,16,128]{2,1,0:T(8,128)(2,1)S(1)} %collective-permute-done.2.peer, bf16[64,16,128]{2,1,0:T(8,128)(2,1)S(1)} %get-tuple-element.184.public_full, ...), custom_call_target="tpu_custom_call" | custom-call | flops 1000000000 | bytes 4194304 | tf_op jit(solution)/shard_map/cond/branch_1_fun/pallas_call | solution.py:360
  45.2 4.5 %collective-permute-done.3.arrived = bf16[40,16,128]{2,1,0:T(8,128)(2,1)S(1)} collective-permute-done((bf16[40,16,128]{2,1,0:T(8,128)(2,1)S(1)}, bf16[40,16,128]{2,1,0:T(8,128)(2,1)S(1)}, u32[]{:S(2)}, u32[]{:S(2)}) %collective-permute-start.3) | collective-permute-done | bytes 163872 | tf_op jit(solution)/shard_map/cond/branch_1_fun/ppermute | solution.py:373
  49.7 1.1 %branch_1_fun.7 = bf16[256,512]{1,0:T(8,128)(2,1)S(1)} custom-call(s32[64]{0:T(128)S(1)} %bitcast_convert_fusion.1.listed, bf16[40,16,128]{2,1,0:T(8,128)(2,1)S(1)} %collective-permute-done.3.arrived, bf16[64,16,128]{2,1,0:T(8,128)(2,1)S(1)} %branch_1_fun.5.filled, f32[256,512]{1,0:T(8,128)S(1)} %get-tuple-element.188.base, ...), custom_call_target="tpu_custom_call" | custom-call | flops 200000000 | bytes 1048576 | tf_op jit(solution)/shard_map/cond/branch_1_fun/pallas_call | solution.py:368
  51.0 0.0 copy-start.4
  51.0 0.7 %copy-done.4 = bf16[1,256,512]{2,1,0:T(8,128)(2,1)} copy-done((bf16[1,256,512]{2,1,0:T(8,128)(2,1)}, bf16[1,256,512]{2,1,0:T(8,128)(2,1)S(1)}, u32[]{:S(2)}) %copy-start.4) | copy-done | bytes 262168
  (2 shorter events, 0.0 us)
Async XLA Ops:
  0.0 14.9 %collective-permute-start.25 = (bf16[128,256]{1,0:T(8,128)(2,1)}, bf16[128,256]{1,0:T(8,128)(2,1)S(1)}, u32[]{:S(2)}, u32[]{:S(2)}) collective-permute-start(bf16[128,256]{1,0:T(8,128)(2,1)} %bitcast.69), channel_id=1, source_target_pairs={{0,1},{1,0},{2,3},{3,2},{4,5},{5,4},{6,7},{7,6},{8,9},{9,8},{10,11... | collective-permute-start | bytes 196616 | tf_op jit(solution)/shard_map/ppermute | solution.py:373
  10.9 0.7 %copy-start.3 = (s32[2]{0:T(128)S(1)}, s32[2]{0:T(128)}, u32[]{:S(2)}) copy-start(s32[2]{0:T(128)} %distances.1) | copy-start | bytes 28
  10.9 0.7 %copy-start.5 = (s32[1,1,40]{2,1,0:T(1,128)S(1)}, s32[1,1,40]{2,1,0:T(1,128)}, u32[]{:S(2)}) copy-start(s32[1,1,40]{2,1,0:T(1,128)} %param.22) | copy-start | bytes 484
  11.6 0.9 %copy-start.2 = (bf16[1,256,512]{2,1,0:T(8,128)(2,1)S(1)}, bf16[1,256,512]{2,1,0:T(8,128)(2,1)}, u32[]{:S(2)}) copy-start(bf16[1,256,512]{2,1,0:T(8,128)(2,1)} %param.20) | copy-start | bytes 786436
  12.5 2.4 %copy-start = (bf16[1,128,256]{2,1,0:T(8,128)(2,1)S(1)}, bf16[1,128,256]{2,1,0:T(8,128)(2,1)}, u32[]{:S(2)}) copy-start(bf16[1,128,256]{2,1,0:T(8,128)(2,1)} %param.17) | copy-start | bytes 196612
  14.9 10.7 %copy-start.1 = (bf16[1,1024,512]{2,1,0:T(8,128)(2,1)S(1)}, bf16[1,1024,512]{2,1,0:T(8,128)(2,1)}, u32[]{:S(2)}) copy-start(bf16[1,1024,512]{2,1,0:T(8,128)(2,1)} %param.18) | copy-start | bytes 3145732
  15.8 12.9 %all-to-all-start = ((bf16[4,2,128,256]{3,2,1,0:T(8,128)(2,1)}), bf16[4,2,128,256]{3,2,1,0:T(8,128)(2,1)S(1)}, u32[]{:S(2)}, u32[]{:S(2)}) async-start(bf16[4,2,128,256]{3,2,1,0:T(8,128)(2,1)} %shard_map.84), calls=%async_computation | async-start | bytes 1048576 | tf_op jit(solution)/shard_map/all_to_all | solution.py:391
  20.6 9.2 %collective-permute-start.24 = (bf16[25,16,128]{2,1,0:T(8,128)(2,1)}, bf16[25,16,128]{2,1,0:T(8,128)(2,1)S(1)}, u32[]{:S(2)}, u32[]{:S(2)}) collective-permute-start(bf16[25,16,128]{2,1,0:T(8,128)(2,1)} %get-tuple-element.326), channel_id=1, source_target_pairs={{0,256},{8,264},{16,272},{24,280},{32,288},{40,296},{48,304},{56,3... | collective-permute-start | bytes 307208 | tf_op jit(solution)/shard_map/ppermute | solution.py:373
  28.7 1.1 %copy-start.6 = (bf16[1,256,512]{2,1,0:T(8,128)(2,1)S(1)}, bf16[1,256,512]{2,1,0:T(8,128)(2,1)}, u32[]{:S(2)}) copy-start(bf16[1,256,512]{2,1,0:T(8,128)(2,1)} %param.19) | copy-start | bytes 786436
  29.9 8.9 %collective-permute-start.2 = (bf16[64,16,128]{2,1,0:T(8,128)(2,1)S(1)}, bf16[64,16,128]{2,1,0:T(8,128)(2,1)S(1)}, u32[]{:S(2)}, u32[]{:S(2)}) collective-permute-start(bf16[64,16,128]{2,1,0:T(8,128)(2,1)S(1)} %get-tuple-element.181), channel_id=1, source_target_pairs={{0,16},{8,24},{16,0},{24,8},{32,48},{40,56},{48,32},{56,40},{64,80... | collective-permute-start | bytes 786440 | tf_op jit(solution)/shard_map/cond/branch_1_fun/ppermute | solution.py:373
  39.4 10.3 %collective-permute-start.3 = (bf16[40,16,128]{2,1,0:T(8,128)(2,1)S(1)}, bf16[40,16,128]{2,1,0:T(8,128)(2,1)S(1)}, u32[]{:S(2)}, u32[]{:S(2)}) collective-permute-start(bf16[40,16,128]{2,1,0:T(8,128)(2,1)S(1)} %get-tuple-element.183), channel_id=1, source_target_pairs={{0,256},{8,264},{16,272},{24,280},{32,288},{40,296},{48,304},{56,3... | collective-permute-start | bytes 491528 | tf_op jit(solution)/shard_map/cond/branch_1_fun/ppermute | solution.py:373
  51.0 0.7 %copy-start.4 = (bf16[1,256,512]{2,1,0:T(8,128)(2,1)}, bf16[1,256,512]{2,1,0:T(8,128)(2,1)S(1)}, u32[]{:S(2)}) copy-start(bf16[1,256,512]{2,1,0:T(8,128)(2,1)S(1)} %get-tuple-element.381) | copy-start | bytes 786436
